TPU v7x, 32 devices: a whole 2x2x4 slice. The times are simulated.
32 devices in a mesh: ops: 4 (over z), sec: 8 (over y, x, core).
Axes of the slice: x: 2, y: 2, z: 4, core: 2. Of those that a mesh axis runs over, the one named last changes fastest.
Arguments:
- wave_vectors: float32 [2, 8, 8, 128, 128], P(None, 'sec'), may hold values from -6 to 6
- left_blocks: float32 [16, 8, 128, 128], P('ops'), may hold values from -0.1875 to 0.1875
- right_blocks: float32 [16, 8, 128, 128], P('ops', 'sec'), may hold values from -0.5 to 0.5
- left_links: int32 [16, 8], P('ops'), may hold values from 0 to 7
- right_links: int32 [16, 8], P('ops', 'sec'), may hold values from 0 to 7, as said below
Outputs:
- sigma: float32 [2, 8, 8, 128, 128], P(None, 'ops', 'sec')
Inputs may be any that keep to these rules, and one draw needn't show every extreme that they name: `right_links`: each entry differs from its column index j by at most one.
All inputs are finite; a program needn't handle non-finite values.
Results may differ from a plain program's by a relative error of at most 0.0001.
Values sent between devices are 32-bit elements; how exact they have to be, the bound alone decides.
A program may use at most 128 MiB of HBM per device.

v0:
```python
import jax
import jax.numpy as jnp
from jax import lax
from jax.sharding import PartitionSpec as P

highest = lax.Precision.HIGHEST


def left_section(col_blocks, left_blocks, left_links):

    def pick_rows(block_set, link_row):
        return jnp.take(block_set, link_row, axis=1)

    picked = jax.vmap(pick_rows, in_axes=(1, 0), out_axes=1)(col_blocks, left_links)
    return jnp.einsum("piab,vpiqbc->viqac", left_blocks, picked, precision=highest)


def on_device(wave_vectors, left_blocks, right_blocks, left_links, right_links):
    right_all, links_all = (
        lax.all_gather(right_blocks, "sec", axis=1, tiled=True),
        lax.all_gather(right_links, "sec", axis=1, tiled=True),
    )

    def pick_cols(link_row):
        return jnp.take(wave_vectors, link_row, axis=2)

    source = jax.vmap(pick_cols, out_axes=1)(links_all)
    products = jnp.einsum("vpqjab,pjcb->vpqjac", source, right_all, precision=highest)
    partial_sum = left_section(
        lax.all_to_all(products, "sec", split_axis=3, concat_axis=2, tiled=True),
        left_blocks,
        left_links,
    )
    summed = lax.psum(partial_sum, "ops")
    row_count = summed.shape[1] // lax.axis_size("ops")
    return lax.dynamic_slice_in_dim(summed, lax.axis_index("ops") * row_count, row_count, 1)


def solution(mesh):
    return jax.shard_map(
        on_device,
        mesh=mesh,
        in_specs=(
            P(None, "sec", None, None, None),
            P("ops", None, None, None),
            P("ops", "sec", None, None),
            P("ops", None),
            P("ops", "sec"),
        ),
        out_specs=P(None, "ops", "sec", None, None),
        check_vma=False,
    )
```

profile of v0, /device:TPU:0, one launch (start us, length us, event | category | flops | bytes accessed | tf_op | source)
XLA Modules:
  0.0 179.1 jit_solution(8387820143911435691)
XLA Ops:
  6.5 0.0 copy-start
  6.5 0.0 all-gather.3.cloned.1.call-start
  6.5 0.7 all-gather.3.cloned.1.call-update
  7.3 10.3 %all-gather = s32[8,1,4]{2,1,0:T(1,128)S(1)} all-gather(s32[1,1,4]{2,1,0:T(1,128)} %bitcast.70), channel_id=1, replica_groups=mesh['ops'=4,'sec'=8] {'sec'}, dimensions={0}, use_global_device_ids=true | all-gather | bytes 144 | tf_op jit(solution)/shard_map/all_gather | solution.py:21
  17.6 0.1 copy.12
  17.7 0.1 reshape.43
  17.8 4.0 %gather_fusion = f32[32,2,128,128]{3,2,1,0:T(8,128)} fusion(f32[2,8,128,128]{3,2,1,0:T(8,128)} %bitcast.67, s32[1024]{0:T(1024)S(1)} %pad_clamp_fusion), kind=kCustom, calls=%fused_computation | custom fusion | bytes 8388736 | tf_op jit(solution)/shard_map/vmap(jit(_take))/gather | solution.py:25
  21.8 18.1 %all-gather.3.cloned.1.call-done = f32[4,8,128,128]{3,2,1,0:T(8,128)} async-done(((f32[4,1,128,128]{3,2,1,0:T(8,128)}), f32[4,8,128,128]{3,2,1,0:T(8,128)}) %all-gather.3.cloned.1.call-update) | async-done | bytes 2097168 | tf_op jit(solution)/shard_map/all_gather | solution.py:20
  39.9 6.0 %fusion.5 = f32[2,4,1,8,128,128]{5,4,0,3,1,2:T(8,128)S(1)} fusion(f32[4,2,1,8,128,128]{5,4,1,3,0,2:T(8,128)} %bitcast.68, f32[4,8,128,128]{3,2,1,0:T(8,128)} %all-gather.3.cloned.1.call-done, pred[4,8]{1,0:T(4,128)(4,1)S(1)} %compare_and_fusion), kind=kOutput, calls=%fused_computation.8 | convolution fusion | flops 1611661312 | bytes 10485792 | tf_op jit(solution)/shard_map/vpqjab,pjcb->vpqjac/dot_general | solution.py:28
  45.9 2.3 %copy.13 = f32[2,4,1,8,128,128]{5,4,0,1,2,3:T(8,128)} copy(f32[2,4,1,8,128,128]{5,4,0,3,1,2:T(8,128)S(1)} %fusion.5) | data formatting | bytes 8388608 | tf_op jit(solution)/shard_map/vpqjab,pjcb->vpqjac/transpose | solution.py:28
  48.1 0.0 copy-start.1
  48.1 4.7 %all-to-all-start = ((f32[2,4,1,8,128,128]{5,4,0,1,2,3:T(8,128)}), f32[2,4,1,8,128,128]{5,4,0,1,2,3:T(8,128)}, u32[]{:S(2)}, u32[]{:S(2)}) async-start(f32[2,4,1,8,128,128]{5,4,0,1,2,3:T(8,128)} %copy.13), calls=%async_computation | async-start | bytes 8388608 | tf_op jit(solution)/shard_map/all_to_all | solution.py:30
  52.8 0.0 all-reduce.2.cloned.1.call-start
  52.9 0.0 copy-done.1
  52.9 0.1 reshape.51
  53.0 0.1 copy.11
  53.1 48.9 %all-to-all-done = f32[2,4,1,8,128,128]{5,4,0,1,2,3:T(8,128)} async-done(((f32[2,4,1,8,128,128]{5,4,0,1,2,3:T(8,128)}), f32[2,4,1,8,128,128]{5,4,0,1,2,3:T(8,128)}, u32[]{:S(2)}, u32[]{:S(2)}) %all-to-all-start) | async-done | bytes 4194336 | tf_op jit(solution)/shard_map/all_to_all | solution.py:30
  101.9 5.0 %gather_fusion.1 = f32[32,2,128,128]{3,2,1,0:T(8,128)} fusion(f32[4,2,8,128,128]{4,3,1,0,2:T(8,128)} %bitcast.17, s32[32]{0:T(128)S(1)} %reshape.51), kind=kCustom, calls=%fused_computation.1 | custom fusion | bytes 8388864 | tf_op jit(solution)/shard_map/vmap(jit(_take))/gather | solution.py:12
  106.9 5.4 %copy.14 = f32[4,8,2,128,128]{3,4,0,2,1:T(8,128)} copy(f32[4,8,2,128,128]{4,3,2,1,0:T(8,128)} %bitcast.69) | data formatting | bytes 8388608 | tf_op jit(solution)/shard_map/vmap(jit(_take))/gather | solution.py:12
  112.3 0.0 copy-done
  112.3 7.0 %fusion.14 = f32[2,8,1,128,128]{3,4,0,1,2:T(8,128)} fusion(f32[4,8,2,128,128]{3,4,0,2,1:T(8,128)} %copy.14, pred[4,8]{0,1:T(8,128)(4,1)S(1)} %copy.11, f32[4,8,128,128]{3,2,1,0:T(8,128)S(1)} %copy-done), kind=kOutput, calls=%fused_computation.15 | convolution fusion | flops 1611661312 | bytes 7340064 | tf_op jit(solution)/shard_map/piab,vpiqbc->viqac/dot_general | solution.py:15
  119.3 0.0 all-reduce.2.cloned.1.call-update
  119.4 51.1 %all-reduce.2.cloned.1.call-done = f32[2,8,1,128,128]{3,4,0,1,2:T(8,128)} async-done(((f32[2,8,1,128,128]{3,4,0,1,2:T(8,128)}), f32[2,8,1,128,128]{3,4,0,1,2:T(8,128)}) %all-reduce.2.cloned.1.call-update) | async-done | bytes 1048592 | tf_op jit(solution)/shard_map/psum | solution.py:34
  170.4 1.0 constant_dynamic-slice_fusion
  171.4 0.8 copy.16
  (5 shorter events, 0.0 us)
Async XLA Ops:
  6.5 105.8 %copy-start = (f32[4,8,128,128]{3,2,1,0:T(8,128)S(1)}, f32[4,8,128,128]{3,2,1,0:T(8,128)}, u32[]{:S(2)}) copy-start(f32[4,8,128,128]{3,2,1,0:T(8,128)} %param.6) | copy-start | bytes 6291460
  6.5 33.4 %all-gather.3.cloned.1.call-start = ((), (), s32[]{:S(2)}) async-start(), calls=%async_computation.1 | async-start | bytes 2359296 | tf_op jit(solution)/shard_map/all_gather | solution.py:20
  48.1 4.7 %copy-start.1 = (s32[4,8]{1,0:T(4,128)S(1)}, s32[4,8]{1,0:T(4,128)}, u32[]{:S(2)}) copy-start(s32[4,8]{1,0:T(4,128)} %param.8) | copy-start | bytes 388
  48.1 53.8 %all-to-all-start = ((f32[2,4,1,8,128,128]{5,4,0,1,2,3:T(8,128)}), f32[2,4,1,8,128,128]{5,4,0,1,2,3:T(8,128)}, u32[]{:S(2)}, u32[]{:S(2)}) async-start(f32[2,4,1,8,128,128]{5,4,0,1,2,3:T(8,128)} %copy.13), calls=%async_computation | async-start | bytes 8388608 | tf_op jit(solution)/shard_map/all_to_all | solution.py:30
  52.8 117.6 %all-reduce.2.cloned.1.call-start = ((), (), s32[]{:S(2)}) async-start(), calls=%async_computation.2 | async-start | bytes 2097152 | tf_op jit(solution)/shard_map/psum | solution.py:34
Sparse Core Ops, SparseCore 0:
  9.3 30.5 all-gather.2
  119.5 50.9 all-reduce.1
where the time goes:
time: 180 us; the launch traced here: 179 us
  waiting for transfers between devices  119 us (66%)
  local copies, waits for them, and re-layouts  18.8 us (10%)
  between operations  13.4 us (7%)
  matrix products  13 us (7%)
  blocking collectives  10.3 us (6%)
  starting transfers between devices  4.72 us (3%)
    psum x1, waiting for transfers between devices, on_device(): summed = lax.psum(partial_sum, 'ops')  51.1 us
    all_to_all x1, waiting for transfers between devices, on_device(): lax.all_to_all(products, 'sec', split_axis=3, concat_axis=2, tiled=True)  48.9 us
    all_gather x1, waiting for transfers between devices, on_device(): lax.all_gather(right_blocks, 'sec', axis=1, tiled=True)  18.1 us
    gather x3, local copies, waits for them, and re-layouts, pick_rows(): return jnp.take(block_set, link_row, axis=1)  10.4 us
    all_gather x1, blocking collectives, on_device(): lax.all_gather(right_links, 'sec', axis=1, tiled=True)  10.3 us
    dot_general x1, matrix products, left_section(): jnp.einsum('piab,vpiqbc->viqac', left_blocks, picked, precision=highest)  7.04 us
    dot_general x1, matrix products, on_device(): jnp.einsum('vpqjab,pjcb->vpqjac', source, right_all, precision=highest)  5.97 us
    all_to_all x1, starting transfers between devices, on_device(): lax.all_to_all(products, 'sec', split_axis=3, concat_axis=2, tiled=True)  4.68 us
  transfers between devices with their start and end apart: 3, of which 3 were waited for; matrix products, arithmetic and copies ran while one was open for 2% of the time, Pallas kernels for 0%

commit v1 on v0

v1 whole, which is shorter than its diff:
```python
import functools

import jax
import jax.numpy as jnp
from jax import lax
from jax.experimental import pallas as pl
from jax.experimental.pallas import tpu as pltpu
from jax.sharding import PartitionSpec as P

f32, bf16 = jnp.float32, jnp.bfloat16
SPAN = 3


def split(x):
    hi = x.astype(bf16)
    return hi, (x - hi.astype(f32)).astype(bf16)


def dot(a, b):
    return lax.dot_general(a, b, (((1,), (0,)), ((), ())), preferred_element_type=f32)


def kernel(ns, no, psi, left, right, llinks, rlinks, out,
           wave, lv, rv, wr, inner, part, got,
           load_sem, own_sem, xs_sem, xr_sem, ss_sem, sr_sem):
    vecs, _, nq, b, _ = psi.shape
    pairs = left.shape[0]
    rows = nq // no
    o, s = lax.axis_index("ops"), lax.axis_index("sec")

    def first(t):
        return jnp.clip(t - 1, 0, nq - SPAN)

    def peer(k):
        return lax.rem(s + k, ns)

    def layer(k):
        return lax.rem(o + k, no)

    loads = [pltpu.make_async_copy(right, rv, load_sem.at[0]),
             pltpu.make_async_copy(left, lv, load_sem.at[1])]
    for c in loads:
        c.start()
    owns = [pltpu.make_async_copy(psi.at[v, 0, pl.ds(first(s), SPAN)], wave.at[v, s], own_sem.at[v])
            for v in range(vecs)]
    for c in owns:
        c.start()

    barrier = pltpu.get_barrier_semaphore()

    @pl.loop(1, ns)
    def _(k):
        pl.semaphore_signal(barrier, inc=1, device_id=(o, peer(k)), device_id_type=pl.DeviceIdType.MESH)

    @pl.loop(1, no)
    def _(k):
        pl.semaphore_signal(barrier, inc=1, device_id=(layer(k), s), device_id_type=pl.DeviceIdType.MESH)

    pl.semaphore_wait(barrier, ns - 1 + no - 1)

    def exchange(v, k):
        t = peer(k)
        return pltpu.make_async_remote_copy(
            src_ref=psi.at[v, 0, pl.ds(first(t), SPAN)], dst_ref=wave.at[v, s],
            send_sem=xs_sem.at[v, k], recv_sem=xr_sem.at[v, k],
            device_id=(o, t), device_id_type=pl.DeviceIdType.MESH)

    for v in range(vecs):
        @pl.loop(1, ns)
        def _(k):
            exchange(v, k).start()

    loads[0].wait()
    for p in range(pairs):
        hi, lo = split(rv[p, 0].T)
        wr[p, :b, :b] = hi
        wr[p, :b, b:] = lo
        wr[p, b:, :b] = hi
        wr[p, b:, b:] = jnp.zeros((b, b), bf16)

    def contract_right(v, q):
        for p in range(pairs):
            d = rlinks[p, 0] - first(s)
            x = jnp.where(d == 0, wave[v, q, 0], jnp.where(d == 1, wave[v, q, 1], wave[v, q, 2]))
            hi, lo = split(x)
            y = dot(jnp.concatenate([hi, lo], axis=1), wr[p])
            hi, lo = split(y[:, :b] + y[:, b:])
            inner[v, p, q, :, :b] = hi
            inner[v, p, q, :, b:] = lo

    def contract_left(v, i):
        pieces = [split(lv[p, i]) for p in range(pairs)]
        picked = jnp.concatenate([inner[v, p, llinks[p, i]] for p in range(pairs)], axis=0)
        y = dot(jnp.concatenate([c[0] for c in pieces], axis=1), picked)
        z = dot(jnp.concatenate([c[1] for c in pieces], axis=1), picked[:, :b])
        return y[:, :b] + y[:, b:] + z

    def scatter(v, k):
        return pltpu.make_async_remote_copy(
            src_ref=part.at[v, k], dst_ref=got.at[v, k],
            send_sem=ss_sem.at[v, k], recv_sem=sr_sem.at[v, k],
            device_id=(layer(k), s), device_id_type=pl.DeviceIdType.MESH)

    for v in range(vecs):
        owns[v].wait()
        contract_right(v, s)

        @pl.loop(1, ns)
        def _(k):
            q = lax.rem(s + ns - k, ns)
            pltpu.make_async_remote_copy(
                src_ref=psi.at[v, 0, pl.ds(0, SPAN)], dst_ref=wave.at[v, q],
                send_sem=xs_sem.at[v, k], recv_sem=xr_sem.at[v, k],
                device_id=(o, q), device_id_type=pl.DeviceIdType.MESH).wait_recv()
            contract_right(v, q)

        if v == 0:
            loads[1].wait()

        @pl.loop(1, no)
        def _(k):
            for r in range(rows):
                part[v, k, r] = contract_left(v, layer(k) * rows + r)
            scatter(v, k).start()

        for r in range(rows):
            part[v, 0, r] = contract_left(v, o * rows + r)

    for v in range(vecs):
        @pl.loop(1, no)
        def _(k):
            scatter(v, k).wait_recv()
        for r in range(rows):
            total = part[v, 0, r]
            for k in range(1, no):
                total = total + got[v, k, r]
            out[v, r, 0] = total

    for v in range(vecs):
        @pl.loop(1, ns)
        def _(k):
            exchange(v, k).wait_send()

        @pl.loop(1, no)
        def _(k):
            scatter(v, k).wait_send()


def on_device(psi, left, right, llinks, rlinks):
    ns, no = lax.axis_size("sec"), lax.axis_size("ops")
    vecs, _, nq, b, _ = psi.shape
    pairs, rows = left.shape[0], nq // no
    shapes = [((vecs, nq, SPAN, b, b), f32), (left.shape, f32), (right.shape, f32),
              ((pairs, 2 * b, 2 * b), bf16), ((vecs, pairs, nq, b, 2 * b), bf16),
              ((vecs, no, rows, b, b), f32), ((vecs, no, rows, b, b), f32)]
    need = sum(jnp.dtype(t).itemsize * functools.reduce(lambda x, y: x * y, d) for d, t in shapes)
    any_, smem, vmem = (pl.BlockSpec(memory_space=m) for m in (pl.ANY, pltpu.SMEM, pltpu.VMEM))
    return pl.pallas_call(
        functools.partial(kernel, ns, no),
        out_shape=jax.ShapeDtypeStruct((vecs, rows, 1, b, b), f32),
        in_specs=[any_, any_, any_, smem, smem],
        out_specs=vmem,
        scratch_shapes=[pltpu.VMEM(d, t) for d, t in shapes] + [
            pltpu.SemaphoreType.DMA((2,)), pltpu.SemaphoreType.DMA((vecs,)),
            pltpu.SemaphoreType.DMA((vecs, ns)), pltpu.SemaphoreType.DMA((vecs, ns)),
            pltpu.SemaphoreType.DMA((vecs, no)), pltpu.SemaphoreType.DMA((vecs, no))],
        compiler_params=pltpu.CompilerParams(
            collective_id=0, has_side_effects=True, vmem_limit_bytes=need + (6 << 20)),
    )(psi, left, right, llinks, rlinks)


def solution(mesh):
    return jax.shard_map(
        on_device,
        mesh=mesh,
        in_specs=(
            P(None, "sec", None, None, None),
            P("ops", None, None, None),
            P("ops", "sec", None, None),
            P("ops", None),
            P("ops", "sec"),
        ),
        out_specs=P(None, "ops", "sec", None, None),
        check_vma=False,
    )
```

time: 180 us -> 58.1 us (0.32)
  waiting for transfers between devices: 119 us -> 0 us
  Pallas kernels: 0 us -> 51.1 us
  between operations: 13.4 us -> 0.01 us
  matrix products: 13 us -> 0 us
  local copies, waits for them, and re-layouts: 18.8 us -> 5.89 us
  blocking collectives: 10.3 us -> 0 us
  starting transfers between devices: 4.72 us -> 0 us
    pallas_call x0 -> x1, Pallas kernels: none -> 51.1 us  [on_device(): pl.pallas_call(functools.partial(kernel, ns, no), out_shape=jax.ShapeDtyp...]
    psum x1 -> x0, waiting for transfers between devices: 51.1 us -> none  [on_device(): summed = lax.psum(partial_sum, 'ops')]
    all_to_all x1 -> x0, waiting for transfers between devices: 48.9 us -> none  [on_device(): lax.all_to_all(products, 'sec', split_axis=3, concat_axis=2, tiled=True)]
    all_gather x1 -> x0, waiting for transfers between devices: 18.1 us -> none  [on_device(): lax.all_gather(right_blocks, 'sec', axis=1, tiled=True)]
    gather x4 -> x0, local copies, waits for them, and re-layouts: 14.4 us -> none  [the longest x3 10.4 us: pick_rows(): return jnp.take(block_set, link_row, axis=1)]
    dot_general x2 -> x0, matrix products: 13 us -> none  [the longest x1 7.04 us: left_section(): jnp.einsum('piab,vpiqbc->viqac', left_blocks, picked, precision=highest)]
    all_gather x1 -> x0, blocking collectives: 10.3 us -> none  [on_device(): lax.all_gather(right_links, 'sec', axis=1, tiled=True)]
    unnamed x4 -> x10, local copies, waits for them, and re-layouts: 0.01 us -> 5.89 us
  transfers between devices with their start and end apart: 3 -> 0, of which waited for: 3 -> 0; matrix products, arithmetic and copies ran while one was open for 2% -> 0% of each run, Pallas kernels for 0% -> 0%
where the time goes in v1:
time: 58.1 us; the launch traced here: 57 us
  Pallas kernels  51.1 us (88%)
  local copies, waits for them, and re-layouts  5.89 us (10%)
    pallas_call x1, Pallas kernels, on_device(): pl.pallas_call(functools.partial(kernel, ns, no), out_shape=jax.ShapeDtyp...  51.1 us
    unnamed x10, local copies, waits for them, and re-layouts  5.89 us

profile of v1, /device:TPU:0, one launch (start us, length us, event | category | flops | bytes accessed | tf_op | source)
XLA Modules:
  0.0 57.0 jit_solution(11156423997333901450)
XLA Ops:
  0.0 0.7 %copy.6.rlinks = s32[4,1]{1,0:T(4,128)S(1)} copy(s32[4,1]{0,1:T(1,128)} %param.9) | data formatting | bytes 32 | tf_op args[4]
  0.7 0.0 copy-start
  0.7 1.6 %copy-done = f32[4,8,128,128]{3,2,1,0:T(8,128)S(1)} copy-done((f32[4,8,128,128]{3,2,1,0:T(8,128)S(1)}, f32[4,8,128,128]{3,2,1,0:T(8,128)}, u32[]{:S(2)}) %copy-start) | copy-done | bytes 2097176
  2.3 0.0 copy-start.1
  2.3 1.2 %copy-done.1 = f32[2,1,8,128,128]{4,3,2,1,0:T(8,128)S(1)} copy-done((f32[2,1,8,128,128]{4,3,2,1,0:T(8,128)S(1)}, f32[2,1,8,128,128]{4,3,2,1,0:T(8,128)}, u32[]{:S(2)}) %copy-start.1) | copy-done | bytes 1048600
  3.6 0.0 copy-start.2
  3.6 0.9 %copy-done.2 = f32[4,1,128,128]{3,2,1,0:T(8,128)S(1)} copy-done((f32[4,1,128,128]{3,2,1,0:T(8,128)S(1)}, f32[4,1,128,128]{3,2,1,0:T(8,128)}, u32[]{:S(2)}) %copy-start.2) | copy-done | bytes 262168
  4.5 0.0 copy-start.3
  4.5 0.7 %copy-done.3 = s32[4,8]{1,0:T(4,128)S(1)} copy-done((s32[4,8]{1,0:T(4,128)S(1)}, s32[4,8]{1,0:T(4,128)}, u32[]{:S(2)}) %copy-start.3) | copy-done | bytes 152
  5.2 51.1 %shard_map.55 = f32[2,2,1,128,128]{4,3,2,1,0:T(8,128)S(1)} custom-call(f32[2,1,8,128,128]{4,3,2,1,0:T(8,128)S(1)} %copy-done.1, f32[4,8,128,128]{3,2,1,0:T(8,128)S(1)} %copy-done, f32[4,1,128,128]{3,2,1,0:T(8,128)S(1)} %copy-done.2, s32[4,8]{1,0:T(4,128)S(1)} %copy-done.3, s32[4,1]{1,0:T(4,128)S(1)} %copy.6.rlinks), custom_call_target="tpu_custom_call" | custom-call | tf_op jit(solution)/shard_map/pallas_call | solution.py:158
  56.3 0.7 %copy.8 = f32[2,2,1,128,128]{4,3,2,1,0:T(8,128)} copy(f32[2,2,1,128,128]{4,3,2,1,0:T(8,128)S(1)} %shard_map.55) | data formatting | bytes 524288
Async XLA Ops:
  0.7 1.6 %copy-start = (f32[4,8,128,128]{3,2,1,0:T(8,128)S(1)}, f32[4,8,128,128]{3,2,1,0:T(8,128)}, u32[]{:S(2)}) copy-start(f32[4,8,128,128]{3,2,1,0:T(8,128)} %left.1) | copy-start | bytes 6291460
  2.3 1.2 %copy-start.1 = (f32[2,1,8,128,128]{4,3,2,1,0:T(8,128)S(1)}, f32[2,1,8,128,128]{4,3,2,1,0:T(8,128)}, u32[]{:S(2)}) copy-start(f32[2,1,8,128,128]{4,3,2,1,0:T(8,128)} %psi.1) | copy-start | bytes 3145732
  3.6 0.9 %copy-start.2 = (f32[4,1,128,128]{3,2,1,0:T(8,128)S(1)}, f32[4,1,128,128]{3,2,1,0:T(8,128)}, u32[]{:S(2)}) copy-start(f32[4,1,128,128]{3,2,1,0:T(8,128)} %right.1) | copy-start | bytes 786436
  4.5 0.7 %copy-start.3 = (s32[4,8]{1,0:T(4,128)S(1)}, s32[4,8]{1,0:T(4,128)}, u32[]{:S(2)}) copy-start(s32[4,8]{1,0:T(4,128)} %llinks.1) | copy-start | bytes 388

commit v2 on v1

--- a/solution.py
+++ b/solution.py
@@ -28,8 +28,8 @@
     rows = nq // no
     o, s = lax.axis_index("ops"), lax.axis_index("sec")
 
-    def first(t):
-        return jnp.clip(t - 1, 0, nq - SPAN)
+    odd = lax.rem(s, 2)
+    mate = s + 1 - 2 * odd
 
     def peer(k):
         return lax.rem(s + k, ns)
@@ -41,10 +41,18 @@
              pltpu.make_async_copy(left, lv, load_sem.at[1])]
     for c in loads:
         c.start()
-    owns = [pltpu.make_async_copy(psi.at[v, 0, pl.ds(first(s), SPAN)], wave.at[v, s], own_sem.at[v])
-            for v in range(vecs)]
-    for c in owns:
-        c.start()
+    def window(t, go):
+        for case, lo, hi in ((t == 0, 1, 3), (t == nq - 1, 0, 2), ((t > 0) & (t < nq - 1), 0, 3)):
+            @pl.when(case)
+            def _():
+                go(pl.ds(t - 1 + lo, hi - lo), pl.ds(lo, hi - lo))
+
+    def own(v, go):
+        window(s, lambda src, dst: go(pltpu.make_async_copy(
+            psi.at[v, 0, src], wave.at[v, s, dst], own_sem.at[v])))
+
+    for v in range(vecs):
+        own(v, lambda c: c.start())
 
     barrier = pltpu.get_barrier_semaphore()
 
@@ -58,17 +66,42 @@
 
     pl.semaphore_wait(barrier, ns - 1 + no - 1)
 
-    def exchange(v, k):
-        t = peer(k)
+    def remote(src, dst, send, recv, to):
         return pltpu.make_async_remote_copy(
-            src_ref=psi.at[v, 0, pl.ds(first(t), SPAN)], dst_ref=wave.at[v, s],
-            send_sem=xs_sem.at[v, k], recv_sem=xr_sem.at[v, k],
-            device_id=(o, t), device_id_type=pl.DeviceIdType.MESH)
-
-    for v in range(vecs):
-        @pl.loop(1, ns)
-        def _(k):
-            exchange(v, k).start()
+            src_ref=src, dst_ref=dst, send_sem=send, recv_sem=recv,
+            device_id=to, device_id_type=pl.DeviceIdType.MESH)
+
+    def partner(k, way):
+        chip = lax.rem(s // 2 + ns // 2 + way * (k // 2), ns // 2)
+        return 2 * chip + lax.rem(s + k, 2)
+
+    def middle(v, row, t, k):
+        return remote(psi.at[v, 0, t], wave.at[v, row, 1], xs_sem.at[v, k, 0], xr_sem.at[v, k, 0], (o, t))
+
+    def outer(v, row, t, k, go):
+        even = lax.rem(t, 2) == 0
+        @pl.when(even & (t > 0))
+        def _():
+            go(remote(psi.at[v, 0, t - 1], wave.at[v, row, 0], xs_sem.at[v, k, 1], xr_sem.at[v, k, 1], (o, t)))
+        @pl.when(jnp.logical_not(even) & (t < nq - 1))
+        def _():
+            go(remote(psi.at[v, 0, t + 1], wave.at[v, row, 2], xs_sem.at[v, k, 1], xr_sem.at[v, k, 1], (o, t)))
+
+    def mated(v, t, row, go):
+        window(t, lambda src, dst: go(remote(
+            psi.at[v, 0, src], wave.at[v, row, dst], xs_sem.at[v, 1, 0], xr_sem.at[v, 1, 0], (o, mate))))
+
+    def forward(v, row, slot):
+        return remote(wave.at[v, row, 1], wave.at[v, row, slot], xs_sem.at[v, row, 2], xr_sem.at[v, row, 2], (o, mate))
+
+    for v in range(vecs):
+        mated(v, mate, s, lambda c: c.start())
+
+        @pl.loop(2, ns)
+        def _(k):
+            t = partner(k, 1)
+            middle(v, s, t, k).start()
+            outer(v, s, t, k, lambda c: c.start())
 
     loads[0].wait()
     for p in range(pairs):
@@ -80,7 +113,7 @@
 
     def contract_right(v, q):
         for p in range(pairs):
-            d = rlinks[p, 0] - first(s)
+            d = rlinks[p, 0] - (s - 1)
             x = jnp.where(d == 0, wave[v, q, 0], jnp.where(d == 1, wave[v, q, 1], wave[v, q, 2]))
             hi, lo = split(x)
             y = dot(jnp.concatenate([hi, lo], axis=1), wr[p])
@@ -102,16 +135,22 @@
             device_id=(layer(k), s), device_id_type=pl.DeviceIdType.MESH)
 
     for v in range(vecs):
-        owns[v].wait()
+        own(v, lambda c: c.wait())
         contract_right(v, s)
-
-        @pl.loop(1, ns)
-        def _(k):
-            q = lax.rem(s + ns - k, ns)
-            pltpu.make_async_remote_copy(
-                src_ref=psi.at[v, 0, pl.ds(0, SPAN)], dst_ref=wave.at[v, q],
-                send_sem=xs_sem.at[v, k], recv_sem=xr_sem.at[v, k],
-                device_id=(o, q), device_id_type=pl.DeviceIdType.MESH).wait_recv()
+        mated(v, s, mate, lambda c: c.wait_recv())
+        contract_right(v, mate)
+
+        @pl.loop(2, ns)
+        def _(k):
+            q = partner(k, -1)
+            middle(v, q, s, k).wait_recv()
+            forward(v, q, 2 * odd).start()
+
+        @pl.loop(2, ns)
+        def _(k):
+            q = partner(k, -1)
+            outer(v, q, s, k, lambda c: c.wait_recv())
+            forward(v, q, 2 - 2 * odd).wait_recv()
             contract_right(v, q)
 
         if v == 0:
@@ -137,9 +176,14 @@
             out[v, r, 0] = total
 
     for v in range(vecs):
-        @pl.loop(1, ns)
-        def _(k):
-            exchange(v, k).wait_send()
+        mated(v, mate, s, lambda c: c.wait_send())
+
+        @pl.loop(2, ns)
+        def _(k):
+            t = partner(k, 1)
+            middle(v, s, t, k).wait_send()
+            outer(v, s, t, k, lambda c: c.wait_send())
+            forward(v, t, 2 * odd).wait_send()
 
         @pl.loop(1, no)
         def _(k):
@@ -162,10 +206,10 @@
         out_specs=vmem,
         scratch_shapes=[pltpu.VMEM(d, t) for d, t in shapes] + [
             pltpu.SemaphoreType.DMA((2,)), pltpu.SemaphoreType.DMA((vecs,)),
-            pltpu.SemaphoreType.DMA((vecs, ns)), pltpu.SemaphoreType.DMA((vecs, ns)),
+            pltpu.SemaphoreType.DMA((vecs, ns, 3)), pltpu.SemaphoreType.DMA((vecs, ns, 3)),
             pltpu.SemaphoreType.DMA((vecs, no)), pltpu.SemaphoreType.DMA((vecs, no))],
         compiler_params=pltpu.CompilerParams(
-            collective_id=0, has_side_effects=True, vmem_limit_bytes=need + (6 << 20)),
+            collective_id=0, has_side_effects=True, vmem_limit_bytes=60 << 20),
     )(psi, left, right, llinks, rlinks)
 
 

time: 58.1 us -> 53.6 us (0.923)
  the two profiles are of different devices: /device:TPU:0 before, /device:TPU:12 now
where the time goes in v2:
time: 53.6 us; the launch traced here: 53.5 us
  Pallas kernels  50.5 us (94%)
  local copies, waits for them, and re-layouts  2.98 us (6%)
    pallas_call x1, Pallas kernels, on_device(): pl.pallas_call(functools.partial(kernel, ns, no), out_shape=jax.ShapeDtyp...  50.5 us
    unnamed x2, local copies, waits for them, and re-layouts  2.98 us

profile of v2, /device:TPU:12, one launch (start us, length us, event | category | flops | bytes accessed | tf_op | source)
XLA Modules:
  0.0 53.5 jit_solution(13333797419034987924)
XLA Ops:
  0.0 1.3 %copy.6.rlinks = s32[4,1]{1,0:T(4,128)} copy(s32[4,1]{0,1:T(1,128)} %param.9) | data formatting | bytes 32 | tf_op args[4]
  1.3 50.5 %shard_map.55 = f32[2,2,1,128,128]{4,3,2,1,0:T(8,128)} custom-call(f32[2,1,8,128,128]{4,3,2,1,0:T(8,128)} %psi.1, f32[4,8,128,128]{3,2,1,0:T(8,128)} %left.1, f32[4,1,128,128]{3,2,1,0:T(8,128)} %right.1, s32[4,8]{1,0:T(4,128)} %llinks.1, s32[4,1]{1,0:T(4,128)} %copy.6.rlinks), custom_call_target="tpu_custom_call" | custom-call | tf_op jit(solution)/shard_map/pallas_call | solution.py:202
  51.8 1.7 %copy.8 = f32[2,2,1,128,128]{4,3,2,1,0:T(8,128)} copy(f32[2,2,1,128,128]{4,3,2,1,0:T(8,128)} %shard_map.55) | data formatting | bytes 524288

commit v3 on v2

v3 whole, which is shorter than its diff:
```python
import functools

import jax
import jax.numpy as jnp
from jax import lax
from jax.experimental import pallas as pl
from jax.experimental.pallas import tpu as pltpu
from jax.sharding import PartitionSpec as P

f32, bf16 = jnp.float32, jnp.bfloat16
SPAN = 3


NEAR = 8


def xor(a, b, n):
    bit, total = 1, 0
    while bit < n:
        total = total + bit * lax.rem(a // bit + b // bit, 2)
        bit *= 2
    return total


def split(x):
    hi = x.astype(bf16)
    return hi, (x - hi.astype(f32)).astype(bf16)


def dot(a, b):
    return lax.dot_general(a, b, (((1,), (0,)), ((), ())), preferred_element_type=f32)


def kernel(ns, no, psi, left, right, links, out,
           wave, lv, rv, wr, inner, part, got, lkv, lk,
           load_sem, own_sem, xs_sem, xr_sem, ss_sem, sr_sem, zs_sem, zr_sem, fs_sem, fr_sem):
    vecs, _, nq, b, _ = psi.shape
    pairs = left.shape[0]
    rows = nq // no
    o, s = lax.axis_index("ops"), lax.axis_index("sec")

    odd = lax.rem(s, 2)
    mate = s + 1 - 2 * odd

    half, hp = no // 2, pairs // 2
    parity = lax.rem(o, 2)
    other = o + 1 - 2 * parity

    def peer(k):
        return lax.rem(s + k, ns)

    def layer(k):
        return lax.rem(o + k, no)

    def kin(k):
        return lax.rem(o // 2 + k, half)

    loads = [pltpu.make_async_copy(right.at[:, 0], rv.at[pl.ds(0, pairs)], load_sem.at[0]),
             pltpu.make_async_copy(links, lk.at[0], load_sem.at[1])]
    loads += [pltpu.make_async_copy(left.at[:, pl.ds((parity + 2 * m) * rows, rows)], lv.at[pl.ds(0, pairs), m],
                                    load_sem.at[2 + m]) for m in range(half)]
    for c in loads:
        c.start()
    def window(t, go):
        for case, lo, hi in ((t == 0, 1, 3), (t == nq - 1, 0, 2), ((t > 0) & (t < nq - 1), 0, 3)):
            @pl.when(case)
            def _():
                go(pl.ds(t - 1 + lo, hi - lo), pl.ds(lo, hi - lo))

    def own(v, go):
        window(s, lambda src, dst: go(pltpu.make_async_copy(
            psi.at[v, 0, src], wave.at[v, s, dst], own_sem.at[v])))

    for v in range(vecs):
        own(v, lambda c: c.start())

    barrier = pltpu.get_barrier_semaphore()

    @pl.loop(1, ns)
    def _(k):
        pl.semaphore_signal(barrier, inc=1, device_id=(o, peer(k)), device_id_type=pl.DeviceIdType.MESH)

    @pl.loop(1, no)
    def _(k):
        pl.semaphore_signal(barrier, inc=1, device_id=(layer(k), s), device_id_type=pl.DeviceIdType.MESH)

    pl.semaphore_wait(barrier, ns - 1 + no - 1)

    def remote(src, dst, send, recv, to):
        return pltpu.make_async_remote_copy(
            src_ref=src, dst_ref=dst, send_sem=send, recv_sem=recv,
            device_id=to, device_id_type=pl.DeviceIdType.MESH)

    def partner(k):
        return xor(s, k, ns)

    near = min(NEAR, ns)

    def direct(row):
        return lax.rem(row + o, 2) == 0

    def middle(v, row, t, k):
        return remote(psi.at[v, 0, t], wave.at[v, row, 1], xs_sem.at[v, k, 0], xr_sem.at[v, k, 0], (o, t))

    def outer(v, row, t, k, go):
        even = lax.rem(t, 2) == 0
        @pl.when(even & (t > 0))
        def _():
            go(remote(psi.at[v, 0, t - 1], wave.at[v, row, 0], xs_sem.at[v, k, 1], xr_sem.at[v, k, 1], (o, t)))
        @pl.when(jnp.logical_not(even) & (t < nq - 1))
        def _():
            go(remote(psi.at[v, 0, t + 1], wave.at[v, row, 2], xs_sem.at[v, k, 1], xr_sem.at[v, k, 1], (o, t)))

    def mated(v, t, row, go):
        window(t, lambda src, dst: go(remote(
            psi.at[v, 0, src], wave.at[v, row, dst], xs_sem.at[v, 1, 0], xr_sem.at[v, 1, 0], (o, mate))))

    def forward(v, row, slot):
        return remote(wave.at[v, row, 1], wave.at[v, row, slot], xs_sem.at[v, row, 2], xr_sem.at[v, row, 2], (o, mate))

    def lift(v, row, go, middle_too=True):
        def one(slot, j):
            go(remote(wave.at[v, row, slot], wave.at[v, row, slot], xs_sem.at[v, row, j], xr_sem.at[v, row, j], (other, s)))
        if middle_too:
            one(1, 3)
        else:
            @pl.when((odd == 0) & (s > 0))
            def _():
                one(0, 4)
            @pl.when((odd == 1) & (s < nq - 1))
            def _():
                one(2, 4)

    mine = pl.ds(pairs + odd * hp, hp)
    across = [remote(right.at[:, 0], rv.at[pl.ds(pairs, pairs)], zs_sem.at[0], zr_sem.at[0], (other, s)),
              remote(links, lkv, zs_sem.at[1], zr_sem.at[1], (other, s))]
    across += [remote(left.at[pl.ds(odd * hp, hp), pl.ds((1 - parity + 2 * m) * rows, rows)], lv.at[mine, m],
                      zs_sem.at[2 + m], zr_sem.at[2 + m], (other, s)) for m in range(half)]
    for c in across:
        c.start()

    def hand(m, which):
        part_of = pl.ds(pairs + which * hp, hp)
        return remote(lv.at[part_of, m], lv.at[part_of, m], fs_sem.at[m], fr_sem.at[m], (o, mate))

    for v in range(vecs):
        @pl.when(direct(s))
        def _():
            @pl.loop(near, ns)
            def _(k):
                t = partner(k)
                middle(v, s, t, k).start()
                outer(v, s, t, k, lambda c: c.start())

        mated(v, mate, s, lambda c: c.start())

        @pl.loop(2, near)
        def _(k):
            t = partner(k)
            middle(v, s, t, k).start()
            outer(v, s, t, k, lambda c: c.start())

    loads[0].wait()
    loads[1].wait()
    across[1].wait_recv()
    arrived = pltpu.make_async_copy(lkv, lk.at[1], load_sem.at[1])
    arrived.start()
    arrived.wait()
    across[0].wait_recv()

    def link(p, i):
        return lk[p // pairs, p % pairs, i]

    for p in range(2 * pairs):
        hi, lo = split(rv[p].T)
        wr[p, :b, :b] = hi
        wr[p, :b, b:] = lo
        wr[p, b:, :b] = hi
        wr[p, b:, b:] = jnp.zeros((b, b), bf16)

    def contract_right(v, q):
        for p in range(2 * pairs):
            d = link(p, nq) - (s - 1)
            x = jnp.where(d == 0, wave[v, q, 0], jnp.where(d == 1, wave[v, q, 1], wave[v, q, 2]))
            hi, lo = split(x)
            y = dot(jnp.concatenate([hi, lo], axis=1), wr[p])
            hi, lo = split(y[:, :b] + y[:, b:])
            inner[p, q, :, :b] = hi
            inner[p, q, :, b:] = lo

    def contract_left(m, r):
        i = (parity + 2 * m) * rows + r
        pieces = [split(lv[p, m, r]) for p in range(2 * pairs)]
        picked = jnp.concatenate([inner[p, link(p, i)] for p in range(2 * pairs)], axis=0)
        y = dot(jnp.concatenate([c[0] for c in pieces], axis=1), picked)
        z = dot(jnp.concatenate([c[1] for c in pieces], axis=1), picked[:, :b])
        return y[:, :b] + y[:, b:] + z

    def scatter(v, k):
        return remote(part.at[v, k], got.at[v, k], ss_sem.at[v, k], sr_sem.at[v, k], (parity + 2 * kin(k), s))

    for v in range(vecs):
        own(v, lambda c: c.wait())
        contract_right(v, s)
        mated(v, s, mate, lambda c: c.wait_recv())
        contract_right(v, mate)

        @pl.loop(near, ns)
        def _(k):
            q = partner(k)

            @pl.when(direct(q))
            def _():
                middle(v, q, s, k).wait_recv()
                lift(v, q, lambda c: c.start())
                forward(v, q, 2 * odd).start()
                outer(v, q, s, k, lambda c: c.wait_recv())
                lift(v, q, lambda c: c.start(), False)

        @pl.loop(2, near)
        def _(k):
            q = partner(k)
            middle(v, q, s, k).wait_recv()
            forward(v, q, 2 * odd).start()

        @pl.loop(2, near)
        def _(k):
            q = partner(k)
            outer(v, q, s, k, lambda c: c.wait_recv())
            forward(v, q, 2 - 2 * odd).wait_recv()
            contract_right(v, q)

        @pl.loop(near, ns)
        def _(k):
            q = partner(k)

            @pl.when(jnp.logical_not(direct(q)))
            def _():
                lift(v, q, lambda c: c.wait_recv())
                forward(v, q, 2 * odd).start()
                lift(v, q, lambda c: c.wait_recv(), False)

        @pl.loop(near, ns)
        def _(k):
            q = partner(k)
            forward(v, q, 2 - 2 * odd).wait_recv()
            contract_right(v, q)

        if v == 0:
            for m in range(half):
                across[2 + m].wait_recv()
                hand(m, odd).start()
            for m in range(half):
                loads[2 + m].wait()
                hand(m, 1 - odd).wait_recv()

        @pl.loop(1, half)
        def _(k):
            for r in range(rows):
                part[v, k, r] = contract_left(kin(k), r)
            scatter(v, k).start()

        for r in range(rows):
            part[v, 0, r] = contract_left(kin(0), r)

    for v in range(vecs):
        @pl.loop(1, half)
        def _(k):
            scatter(v, k).wait_recv()
        for r in range(rows):
            total = part[v, 0, r]
            for k in range(1, half):
                total = total + got[v, k, r]
            out[v, r, 0] = total

    for c in across:
        c.wait_send()
    for m in range(half):
        hand(m, odd).wait_send()

    for v in range(vecs):
        mated(v, mate, s, lambda c: c.wait_send())

        @pl.loop(2, near)
        def _(k):
            t = partner(k)
            middle(v, s, t, k).wait_send()
            outer(v, s, t, k, lambda c: c.wait_send())
            forward(v, t, 2 * odd).wait_send()

        @pl.loop(near, ns)
        def _(k):
            t = partner(k)
            forward(v, t, 2 * odd).wait_send()

            @pl.when(direct(s))
            def _():
                middle(v, s, t, k).wait_send()
                outer(v, s, t, k, lambda c: c.wait_send())

            @pl.when(direct(t))
            def _():
                lift(v, t, lambda c: c.wait_send())
                lift(v, t, lambda c: c.wait_send(), False)

        @pl.loop(1, half)
        def _(k):
            scatter(v, k).wait_send()


def on_device(psi, left, right, llinks, rlinks):
    ns, no = lax.axis_size("sec"), lax.axis_size("ops")
    vecs, _, nq, b, _ = psi.shape
    pairs, rows, half = left.shape[0], nq // no, no // 2
    links = jnp.concatenate([llinks, rlinks], axis=1)
    links = jnp.pad(links, ((0, -pairs % 8), (0, -(nq + 1) % 128)))
    shapes = [((vecs, nq, SPAN, b, b), f32), ((2 * pairs, half, rows, b, b), f32), ((2 * pairs, b, b), f32),
              ((2 * pairs, 2 * b, 2 * b), bf16), ((2 * pairs, nq, b, 2 * b), bf16),
              ((vecs, half, rows, b, b), f32), ((vecs, half, rows, b, b), f32), (links.shape, jnp.int32)]
    any_, vmem = (pl.BlockSpec(memory_space=m) for m in (pl.ANY, pltpu.VMEM))
    dma = pltpu.SemaphoreType.DMA
    return pl.pallas_call(
        functools.partial(kernel, ns, no),
        out_shape=jax.ShapeDtypeStruct((vecs, rows, 1, b, b), f32),
        in_specs=[any_] * 4,
        out_specs=vmem,
        scratch_shapes=[pltpu.VMEM(d, t) for d, t in shapes] + [
            pltpu.SMEM((2, *links.shape), jnp.int32), dma((2 + half,)), dma((vecs,)),
            dma((vecs, ns, 5)), dma((vecs, ns, 5)), dma((vecs, half)), dma((vecs, half)),
            dma((2 + half,)), dma((2 + half,)), dma((half,)), dma((half,))],
        compiler_params=pltpu.CompilerParams(
            collective_id=0, has_side_effects=True, vmem_limit_bytes=60 << 20),
    )(psi, left, right, links)


def solution(mesh):
    return jax.shard_map(
        on_device,
        mesh=mesh,
        in_specs=(
            P(None, "sec", None, None, None),
            P("ops", None, None, None),
            P("ops", "sec", None, None),
            P("ops", None),
            P("ops", "sec"),
        ),
        out_specs=P(None, "ops", "sec", None, None),
        check_vma=False,
    )
```

time: 53.6 us -> 46.6 us (0.87)
  the two profiles are of different devices: /device:TPU:12 before, /device:TPU:0 now
where the time goes in v3:
time: 46.6 us; the launch traced here: 46.5 us
  Pallas kernels  42.7 us (92%)
  local copies, waits for them, and re-layouts  3.01 us (6%)
  other arithmetic  0.75 us (2%)
    pallas_call x1, Pallas kernels, on_device(): pl.pallas_call(functools.partial(kernel, ns, no), out_shape=jax.ShapeDtyp...  42.7 us
    unnamed x2, local copies, waits for them, and re-layouts  2.41 us

profile of v3, /device:TPU:0, one launch (start us, length us, event | category | flops | bytes accessed | tf_op | source)
XLA Modules:
  0.0 46.5 jit_solution(1809136027284865424)
XLA Ops:
  0.0 0.7 %copy.6 = s32[4,1]{1,0:T(4,128)S(1)} copy(s32[4,1]{0,1:T(1,128)} %param.9) | data formatting | bytes 32 | tf_op args[4]
  0.7 0.8 %pad_add_fusion = s32[4,9]{1,0:T(4,128)S(1)} fusion(s32[4,1]{1,0:T(4,128)S(1)} %copy.6, s32[4,8]{1,0:T(4,128)} %param.8), kind=kLoop, calls=%fused_computation | loop fusion | flops 36 | bytes 288 | tf_op jit(solution)/shard_map/concatenate | solution.py:315
  1.5 0.6 %pad.4.links = s32[8,128]{1,0:T(8,128)} pad(s32[4,9]{1,0:T(4,128)S(1)} %pad_add_fusion, s32[]{:T(128)} %constant.0.clone.1), padding=0_4x0_119 | pad | bytes 4244 | tf_op jit(solution)/shard_map/jit(_pad)/pad | solution.py:316
  2.1 42.7 %shard_map.55 = f32[2,2,1,128,128]{4,3,2,1,0:T(8,128)} custom-call(f32[2,1,8,128,128]{4,3,2,1,0:T(8,128)} %psi.1, f32[4,8,128,128]{3,2,1,0:T(8,128)} %left.1, f32[4,1,128,128]{3,2,1,0:T(8,128)} %right.1, s32[8,128]{1,0:T(8,128)} %pad.4.links), custom_call_target="tpu_custom_call" | custom-call | tf_op jit(solution)/shard_map/pallas_call | solution.py:322
  44.8 1.7 %copy.8 = f32[2,2,1,128,128]{4,3,2,1,0:T(8,128)} copy(f32[2,2,1,128,128]{4,3,2,1,0:T(8,128)} %shard_map.55) | data formatting | bytes 524288

commit v4 on v3

--- a/solution.py
+++ b/solution.py
@@ -31,8 +31,8 @@
     return lax.dot_general(a, b, (((1,), (0,)), ((), ())), preferred_element_type=f32)
 
 
-def kernel(ns, no, psi, left, right, links, out,
-           wave, lv, rv, wr, inner, part, got, lkv, lk,
+def kernel(ns, no, psi, left, right, llinks, rlinks, out,
+           wave, lv, rv, wr, inner, part, got, links, lkv, lk,
            load_sem, own_sem, xs_sem, xr_sem, ss_sem, sr_sem, zs_sem, zr_sem, fs_sem, fr_sem):
     vecs, _, nq, b, _ = psi.shape
     pairs = left.shape[0]
@@ -55,6 +55,9 @@
     def kin(k):
         return lax.rem(o // 2 + k, half)
 
+    links[...] = jnp.zeros_like(links)
+    links[:pairs, :nq] = llinks[...]
+    links[pairs:pairs + 1, :pairs] = rlinks[...]
     loads = [pltpu.make_async_copy(right.at[:, 0], rv.at[pl.ds(0, pairs)], load_sem.at[0]),
              pltpu.make_async_copy(links, lk.at[0], load_sem.at[1])]
     loads += [pltpu.make_async_copy(left.at[:, pl.ds((parity + 2 * m) * rows, rows)], lv.at[pl.ds(0, pairs), m],
@@ -131,17 +134,18 @@
             def _():
                 one(2, 4)
 
+    turns = [*range(1, half), 0]
     mine = pl.ds(pairs + odd * hp, hp)
     across = [remote(right.at[:, 0], rv.at[pl.ds(pairs, pairs)], zs_sem.at[0], zr_sem.at[0], (other, s)),
-              remote(links, lkv, zs_sem.at[1], zr_sem.at[1], (other, s))]
-    across += [remote(left.at[pl.ds(odd * hp, hp), pl.ds((1 - parity + 2 * m) * rows, rows)], lv.at[mine, m],
-                      zs_sem.at[2 + m], zr_sem.at[2 + m], (other, s)) for m in range(half)]
+              remote(links, lkv, zs_sem.at[half + 1], zr_sem.at[half + 1], (other, s))]
+    across += [remote(left.at[pl.ds(odd * hp, hp), pl.ds((1 - parity + 2 * kin(m)) * rows, rows)], lv.at[mine, kin(m)],
+                      zs_sem.at[1 + m], zr_sem.at[1 + m], (other, s)) for m in turns]
     for c in across:
         c.start()
 
     def hand(m, which):
         part_of = pl.ds(pairs + which * hp, hp)
-        return remote(lv.at[part_of, m], lv.at[part_of, m], fs_sem.at[m], fr_sem.at[m], (o, mate))
+        return remote(lv.at[part_of, kin(m)], lv.at[part_of, kin(m)], fs_sem.at[m], fr_sem.at[m], (o, mate))
 
     for v in range(vecs):
         @pl.when(direct(s))
@@ -168,8 +172,11 @@
     arrived.wait()
     across[0].wait_recv()
 
-    def link(p, i):
+    def left_link(p, i):
         return lk[p // pairs, p % pairs, i]
+
+    def right_link(p):
+        return lk[p // pairs, pairs, p % pairs]
 
     for p in range(2 * pairs):
         hi, lo = split(rv[p].T)
@@ -180,7 +187,7 @@
 
     def contract_right(v, q):
         for p in range(2 * pairs):
-            d = link(p, nq) - (s - 1)
+            d = right_link(p) - (s - 1)
             x = jnp.where(d == 0, wave[v, q, 0], jnp.where(d == 1, wave[v, q, 1], wave[v, q, 2]))
             hi, lo = split(x)
             y = dot(jnp.concatenate([hi, lo], axis=1), wr[p])
@@ -191,7 +198,7 @@
     def contract_left(m, r):
         i = (parity + 2 * m) * rows + r
         pieces = [split(lv[p, m, r]) for p in range(2 * pairs)]
-        picked = jnp.concatenate([inner[p, link(p, i)] for p in range(2 * pairs)], axis=0)
+        picked = jnp.concatenate([inner[p, left_link(p, i)] for p in range(2 * pairs)], axis=0)
         y = dot(jnp.concatenate([c[0] for c in pieces], axis=1), picked)
         z = dot(jnp.concatenate([c[1] for c in pieces], axis=1), picked[:, :b])
         return y[:, :b] + y[:, b:] + z
@@ -246,22 +253,18 @@
             forward(v, q, 2 - 2 * odd).wait_recv()
             contract_right(v, q)
 
-        if v == 0:
-            for m in range(half):
-                across[2 + m].wait_recv()
-                hand(m, odd).start()
-            for m in range(half):
-                loads[2 + m].wait()
-                hand(m, 1 - odd).wait_recv()
-
-        @pl.loop(1, half)
-        def _(k):
+        for place, k in enumerate(turns):
+            if v == 0:
+                across[2 + place].wait_recv()
+                hand(k, odd).start()
+                if place == 0:
+                    for m in range(half):
+                        loads[2 + m].wait()
+                hand(k, 1 - odd).wait_recv()
             for r in range(rows):
                 part[v, k, r] = contract_left(kin(k), r)
-            scatter(v, k).start()
-
-        for r in range(rows):
-            part[v, 0, r] = contract_left(kin(0), r)
+            if k > 0:
+                scatter(v, k).start()
 
     for v in range(vecs):
         @pl.loop(1, half)
@@ -312,25 +315,24 @@
     ns, no = lax.axis_size("sec"), lax.axis_size("ops")
     vecs, _, nq, b, _ = psi.shape
     pairs, rows, half = left.shape[0], nq // no, no // 2
-    links = jnp.concatenate([llinks, rlinks], axis=1)
-    links = jnp.pad(links, ((0, -pairs % 8), (0, -(nq + 1) % 128)))
+    table = (pairs + 8 - pairs % 8, nq + -nq % 128)
     shapes = [((vecs, nq, SPAN, b, b), f32), ((2 * pairs, half, rows, b, b), f32), ((2 * pairs, b, b), f32),
               ((2 * pairs, 2 * b, 2 * b), bf16), ((2 * pairs, nq, b, 2 * b), bf16),
-              ((vecs, half, rows, b, b), f32), ((vecs, half, rows, b, b), f32), (links.shape, jnp.int32)]
+              ((vecs, half, rows, b, b), f32), ((vecs, half, rows, b, b), f32), (table, jnp.int32), (table, jnp.int32)]
     any_, vmem = (pl.BlockSpec(memory_space=m) for m in (pl.ANY, pltpu.VMEM))
     dma = pltpu.SemaphoreType.DMA
     return pl.pallas_call(
         functools.partial(kernel, ns, no),
         out_shape=jax.ShapeDtypeStruct((vecs, rows, 1, b, b), f32),
-        in_specs=[any_] * 4,
+        in_specs=[any_] * 3 + [vmem] * 2,
         out_specs=vmem,
         scratch_shapes=[pltpu.VMEM(d, t) for d, t in shapes] + [
-            pltpu.SMEM((2, *links.shape), jnp.int32), dma((2 + half,)), dma((vecs,)),
+            pltpu.SMEM((2, *table), jnp.int32), dma((2 + half,)), dma((vecs,)),
             dma((vecs, ns, 5)), dma((vecs, ns, 5)), dma((vecs, half)), dma((vecs, half)),
             dma((2 + half,)), dma((2 + half,)), dma((half,)), dma((half,))],
         compiler_params=pltpu.CompilerParams(
             collective_id=0, has_side_effects=True, vmem_limit_bytes=60 << 20),
-    )(psi, left, right, links)
+    )(psi, left, right, llinks, rlinks.T)
 
 
 def solution(mesh):

time: 46.6 us -> 43.7 us (0.938)
  local copies, waits for them, and re-layouts: 3.01 us -> 1.67 us
  Pallas kernels: 42.7 us -> 41.8 us
  other arithmetic: 0.75 us -> 0 us
    pallas_call x1, Pallas kernels: 42.7 us -> 41.8 us  [on_device(): pl.pallas_call(functools.partial(kernel, ns, no), out_shape=jax.ShapeDtyp...]
    concatenate x1 -> x0, other arithmetic: 0.75 us -> none  [on_device(): links = jnp.concatenate([llinks, rlinks], axis=1)]
    unnamed x2 -> x1, local copies, waits for them, and re-layouts: 2.41 us -> 1.67 us
    pad x1 -> x0, local copies, waits for them, and re-layouts: 0.6 us -> none  [on_device(): links = jnp.pad(links, ((0, -pairs % 8), (0, -(nq + 1) % 128)))]
where the time goes in v4:
time: 43.7 us; the launch traced here: 43.5 us
  Pallas kernels  41.8 us (96%)
  local copies, waits for them, and re-layouts  1.67 us (4%)
    pallas_call x1, Pallas kernels, on_device(): pl.pallas_call(functools.partial(kernel, ns, no), out_shape=jax.ShapeDtyp...  41.8 us
    unnamed x1, local copies, waits for them, and re-layouts  1.67 us

profile of v4, /device:TPU:0, one launch (start us, length us, event | category | flops | bytes accessed | tf_op | source)
XLA Modules:
  0.0 43.5 jit_solution(15275823602235096932)
XLA Ops:
  0.0 41.8 %shard_map.55 = f32[2,2,1,128,128]{4,3,2,1,0:T(8,128)} custom-call(f32[2,1,8,128,128]{4,3,2,1,0:T(8,128)} %psi.1, f32[4,8,128,128]{3,2,1,0:T(8,128)} %left.1, f32[4,1,128,128]{3,2,1,0:T(8,128)} %right.1, s32[4,8]{1,0:T(4,128)} %llinks.1, s32[1,4]{1,0:T(1,128)} %bitcast.1), custom_call_target="tpu_custom_call" | custom-call | tf_op jit(solution)/shard_map/pallas_call | solution.py:324
  41.8 1.7 %copy.7 = f32[2,2,1,128,128]{4,3,2,1,0:T(8,128)} copy(f32[2,2,1,128,128]{4,3,2,1,0:T(8,128)} %shard_map.55) | data formatting | bytes 524288

commit v5 on v4

--- a/solution.py
+++ b/solution.py
@@ -203,8 +203,8 @@
         z = dot(jnp.concatenate([c[1] for c in pieces], axis=1), picked[:, :b])
         return y[:, :b] + y[:, b:] + z
 
-    def scatter(v, k):
-        return remote(part.at[v, k], got.at[v, k], ss_sem.at[v, k], sr_sem.at[v, k], (parity + 2 * kin(k), s))
+    def scatter(v, k, r):
+        return remote(part.at[v, k, r], got.at[v, k, r], ss_sem.at[v, k, r], sr_sem.at[v, k, r], (parity + 2 * kin(k), s))
 
     for v in range(vecs):
         own(v, lambda c: c.wait())
@@ -263,14 +263,13 @@
                 hand(k, 1 - odd).wait_recv()
             for r in range(rows):
                 part[v, k, r] = contract_left(kin(k), r)
-            if k > 0:
-                scatter(v, k).start()
-
-    for v in range(vecs):
-        @pl.loop(1, half)
-        def _(k):
-            scatter(v, k).wait_recv()
+                if k > 0:
+                    scatter(v, k, r).start()
+
+    for v in range(vecs):
         for r in range(rows):
+            for k in range(1, half):
+                scatter(v, k, r).wait_recv()
             total = part[v, 0, r]
             for k in range(1, half):
                 total = total + got[v, k, r]
@@ -308,7 +307,8 @@
 
         @pl.loop(1, half)
         def _(k):
-            scatter(v, k).wait_send()
+            for r in range(rows):
+                scatter(v, k, r).wait_send()
 
 
 def on_device(psi, left, right, llinks, rlinks):
@@ -328,7 +328,7 @@
         out_specs=vmem,
         scratch_shapes=[pltpu.VMEM(d, t) for d, t in shapes] + [
             pltpu.SMEM((2, *table), jnp.int32), dma((2 + half,)), dma((vecs,)),
-            dma((vecs, ns, 5)), dma((vecs, ns, 5)), dma((vecs, half)), dma((vecs, half)),
+            dma((vecs, ns, 5)), dma((vecs, ns, 5)), dma((vecs, half, rows)), dma((vecs, half, rows)),
             dma((2 + half,)), dma((2 + half,)), dma((half,)), dma((half,))],
         compiler_params=pltpu.CompilerParams(
             collective_id=0, has_side_effects=True, vmem_limit_bytes=60 << 20),

time: 43.7 us -> 43.6 us (level)
  no operation moved by 1% of the time
where the time goes in v5:
time: 43.6 us; the launch traced here: 43.4 us
  Pallas kernels  41.8 us (96%)
  local copies, waits for them, and re-layouts  1.67 us (4%)
    pallas_call x1, Pallas kernels, on_device(): pl.pallas_call(functools.partial(kernel, ns, no), out_shape=jax.ShapeDtyp...  41.8 us
    unnamed x1, local copies, waits for them, and re-layouts  1.67 us

profile of v5, /device:TPU:0, one launch (start us, length us, event | category | flops | bytes accessed | tf_op | source)
XLA Modules:
  0.0 43.4 jit_solution(18088069617917801783)
XLA Ops:
  0.0 41.8 %shard_map.55 = f32[2,2,1,128,128]{4,3,2,1,0:T(8,128)} custom-call(f32[2,1,8,128,128]{4,3,2,1,0:T(8,128)} %psi.1, f32[4,8,128,128]{3,2,1,0:T(8,128)} %left.1, f32[4,1,128,128]{3,2,1,0:T(8,128)} %right.1, s32[4,8]{1,0:T(4,128)} %llinks.1, s32[1,4]{1,0:T(1,128)} %bitcast.1), custom_call_target="tpu_custom_call" | custom-call | tf_op jit(solution)/shard_map/pallas_call | solution.py:324
  41.8 1.7 %copy.7 = f32[2,2,1,128,128]{4,3,2,1,0:T(8,128)} copy(f32[2,2,1,128,128]{4,3,2,1,0:T(8,128)} %shard_map.55) | data formatting | bytes 524288
